TPU v7x, 256 devices: a whole 4x4x8 slice. The times are simulated.
256 devices in a mesh: island: 8 (over y_hi, x), fsdp: 32 (over y_lo, z, core).
Axes of the slice: x: 4, y: 4 (y_hi: 2, y_lo: 2; y = y_hi * 2 + y_lo), z: 8, core: 2. Of those that a mesh axis runs over, the one named last changes fastest.
Arguments:
- hidden_in: bfloat16 [8, 8192, 8192], P('island', 'fsdp'), may hold values from -6 to 6
- norm_gain: bfloat16 [8, 8192], P('island'), may hold values from 0.5 to 2
- key_weight: bfloat16 [8, 8192, 512], P('island', 'fsdp'), may hold values from -0.0625 to 0.0625
- key_cotangent: bfloat16 [8, 8192, 512], P('island', 'fsdp'), may hold values from -6 to 6
- frag_global: float32 [8192, 512], P('fsdp'), may hold values from -6 to 6
- frag_moment: float32 [8192, 512], P('fsdp'), may hold values from -4 to 4
- frag_local: bfloat16 [8, 8192, 512], P('island', 'fsdp'), may hold values from -6 to 6
Outputs:
- keys: bfloat16 [8, 8192, 512], P('island', 'fsdp')
- grad_in: bfloat16 [8, 8192, 8192], P('island', 'fsdp')
- grad_w: float32 [8, 8192, 512], P('island', 'fsdp')
- new_global: float32 [8192, 512], P('fsdp')
- new_moment: float32 [8192, 512], P('fsdp')
- new_local: bfloat16 [8, 8192, 512], P('island', 'fsdp')
All inputs are finite; a program needn't handle non-finite values.
Results may differ from a plain program's by a relative error of at most 0.0049.
Values may be sent and summed in bfloat16 or wider, within the bound.
A program may use at most 128 MiB of HBM per device.

v0:
```python
import jax
import jax.numpy as jnp
from jax import lax
from jax.sharding import PartitionSpec as P

epsilon = 1e-05
outer_rate = 0.7
outer_momentum = 0.9
mix_weight = 0.5


def nesterov(pseudo, moment, params):
    new_moment = outer_momentum * moment + pseudo
    new_params = params - outer_rate * (pseudo + outer_momentum * new_moment)
    return (new_moment, new_params)


def body(hidden_in, norm_gain, key_weight, key_cotangent, frag_global, frag_moment, frag_local):
    hidden_f = hidden_in[0].astype(jnp.float32)
    gain_f = norm_gain[0].astype(jnp.float32)
    scale = lax.rsqrt(jnp.mean(hidden_f * hidden_f, axis=-1, keepdims=True) + epsilon)
    normed = (hidden_f * scale * gain_f).astype(jnp.bfloat16)
    cotangent = key_cotangent[0]
    gathered = lax.all_gather(key_weight, "fsdp", axis=1, tiled=True)[0]
    key_sum = jnp.dot(normed, gathered, preferred_element_type=jnp.float32)
    back = jnp.einsum("tk,dk->td", cotangent, gathered, preferred_element_type=jnp.float32)
    keys = key_sum.astype(jnp.bfloat16)
    upper = back * gain_f
    inner = jnp.mean(upper * hidden_f, axis=-1, keepdims=True)
    grad_in = (scale * upper - hidden_f * scale * scale * scale * inner).astype(jnp.bfloat16)
    grad_w = lax.psum_scatter(
        jnp.einsum("td,tk->dk", normed, cotangent, preferred_element_type=jnp.float32),
        "fsdp",
        scatter_dimension=0,
        tiled=True,
    )
    islands = lax.axis_size("island")
    local_f = frag_local[0].astype(jnp.float32)
    difference = frag_global - local_f
    summed = lax.psum(difference, "island")
    new_moment, new_global = nesterov(summed / islands, frag_moment, frag_global)
    new_local = (mix_weight * local_f + (1.0 - mix_weight) * new_global).astype(jnp.bfloat16)
    return (keys[None], grad_in[None], grad_w[None], new_global, new_moment, new_local[None])


def solution(mesh):
    in_specs = (
        P("island", "fsdp", None),
        P("island", None),
        P("island", "fsdp", None),
        P("island", "fsdp", None),
        P("fsdp", None),
        P("fsdp", None),
        P("island", "fsdp", None),
    )
    out_specs = (
        P("island", "fsdp", None),
        P("island", "fsdp", None),
        P("island", "fsdp", None),
        P("fsdp", None),
        P("fsdp", None),
        P("island", "fsdp", None),
    )
    return jax.shard_map(body, mesh=mesh, in_specs=in_specs, out_specs=out_specs, check_vma=False)
```

profile of v0, /device:TPU:2, one launch (start us, length us, event | category | flops | bytes accessed | tf_op | source)
XLA Modules:
  0.0 257.9 jit_solution(416443387016718516)
XLA Ops:
  8.0 0.0 copy-start
  8.0 0.0 all-gather.2.cloned.1.call-start
  8.1 0.7 all-gather.2.cloned.1.call-update
  8.7 0.0 all-reduce.2.cloned.1.call-start
  8.8 2.0 convert_subtract_fusion
  10.8 0.0 all-reduce.2.cloned.1.call-update
  10.8 0.0 reduce-scatter.2.cloned.1.call-start
  10.8 0.8 mul.110
  11.6 74.3 %all-gather.2.cloned.1.call-done = bf16[1,8192,512]{2,1,0:T(8,128)(2,1)} async-done(((bf16[1,256,512]{2,1,0:T(8,128)(2,1)}), bf16[1,8192,512]{2,1,0:T(8,128)(2,1)}) %all-gather.2.cloned.1.call-update) | async-done | bytes 8388624 | tf_op jit(solution)/shard_map/all_gather | solution.py:24
  86.0 0.0 copy-done
  86.0 0.0 copy-start.1
  86.0 11.9 %fusion.9 = (f32[256]{0:T(256)S(1)}, f32[256]{0:T(256)S(1)}, f32[256,8192]{1,0:T(8,128)}) fusion(bf16[1,256,8192]{2,1,0:T(8,128)(2,1)} %param.7, f32[8192]{0:T(1024)S(1)} %bitcast.62, bf16[1,8192,512]{2,1,0:T(8,128)(2,1)} %all-gather.2.cloned.1.call-done, bf16[1,256,512]{2,1,0:T(8,128)(2,1)S(1)} %copy-done), kind=kOutput, calls=%fused_computation.12 | convolution fusion | flops 2160066048 | bytes 21268480 | tf_op jit(solution)/shard_map/tk,dk->td/dot_general | solution.py:26
  97.9 0.0 copy-done.1
  97.9 8.3 %fusion.20 = f32[8192,512]{1,0:T(8,128)} fusion(bf16[1,256,8192]{2,1,0:T(8,128)(2,1)S(1)} %copy-done.1, f32[8192]{0:T(1024)S(1)} %bitcast.63, f32[256]{0:T(256)S(1)} %add_rsqrt_fusion, bf16[1,256,512]{2,1,0:T(8,128)(2,1)S(1)} %copy-done), kind=kOutput, calls=%fused_computation.21 | convolution fusion | flops 2155872256 | bytes 21267456 | tf_op jit(solution)/shard_map/td,tk->dk/dot_general | solution.py:32
  106.2 0.0 copy-start.3
  106.2 0.0 copy-start.4
  106.2 0.0 copy-start.5
  106.2 0.0 reduce-scatter.2.cloned.1.call-update
  106.2 0.0 all-reduce.2.cloned.1.call-done
  106.3 1.0 copy-done.3
  107.3 0.1 copy-done.4
  107.3 0.2 copy-done.5
  107.5 0.0 slice-start
  107.5 2.4 fusion.30
  109.9 0.0 copy-start.2
  109.9 0.0 slice-start.1
  109.9 7.9 %fusion.23 = bf16[1,256,512]{2,1,0:T(8,128)(2,1)} fusion(bf16[1,8192,512]{2,1,0:T(8,128)(2,1)} %all-gather.2.cloned.1.call-done, bf16[1,256,8192]{2,1,0:T(8,128)(2,1)} %param.7, f32[8192]{0:T(1024)S(1)} %bitcast.64, f32[256]{0:T(256)S(1)} %add_rsqrt_fusion), kind=kOutput, calls=%fused_computation.22 | convolution fusion | flops 2156003328 | bytes 12878848 | tf_op jit(solution)/shard_map/dot_general | solution.py:25
  117.8 0.0 slice-done
  117.8 0.0 copy-done.2
  117.8 0.0 slice-done.1
  117.8 3.7 %fusion.16 = bf16[1,256,8192]{2,1,0:T(8,128)(2,1)} fusion(bf16[1,256,8192]{2,1,0:T(8,128)(2,1)S(1)} %copy-done.2, f32[256,8192]{1,0:T(8,128)S(1)} %bitcast.61, f32[256]{0:T(256)S(1)} %broadcast_multiply_fusion, f32[256]{0:T(256)S(1)} %add_rsqrt_fusion), kind=kLoop, calls=%fused_computation.19 | loop fusion | flops 16777216 | bytes 16779264 | tf_op jit(solution)/shard_map/broadcast_in_dim | solution.py:43
  121.6 128.9 %reduce-scatter.2.cloned.1.call-done = f32[256,512]{1,0:T(8,128)} async-done(((f32[8192,512]{1,0:T(8,128)}), f32[256,512]{1,0:T(8,128)}) %reduce-scatter.2.cloned.1.call-update) | async-done | bytes 524304 | tf_op jit(solution)/shard_map/reduce_scatter | solution.py:31
  (3 shorter events, 0.0 us)
Async XLA Ops:
  8.0 78.0 %copy-start = (bf16[1,256,512]{2,1,0:T(8,128)(2,1)S(1)}, bf16[1,256,512]{2,1,0:T(8,128)(2,1)}, u32[]{:S(2)}) copy-start(bf16[1,256,512]{2,1,0:T(8,128)(2,1)} %param.10) | copy-start | bytes 786436
  8.0 78.0 %all-gather.2.cloned.1.call-start = ((), (), s32[]{:S(2)}) async-start(), calls=%async_computation.1 | async-start | bytes 8650752 | tf_op jit(solution)/shard_map/all_gather | solution.py:24
  8.7 97.5 %all-reduce.2.cloned.1.call-start = ((), (), s32[]{:S(2)}) async-start(), calls=%async_computation.3 | async-start | bytes 1048576 | tf_op jit(solution)/shard_map/psum | solution.py:40
  10.8 239.6 %reduce-scatter.2.cloned.1.call-start = ((), (), s32[]{:S(2)}) async-start(), calls=%async_computation.2 | async-start | bytes 17301504 | tf_op jit(solution)/shard_map/reduce_scatter | solution.py:31
  86.0 12.0 %copy-start.1 = (bf16[1,256,8192]{2,1,0:T(8,128)(2,1)S(1)}, bf16[1,256,8192]{2,1,0:T(8,128)(2,1)}, u32[]{:S(2)}) copy-start(bf16[1,256,8192]{2,1,0:T(8,128)(2,1)} %param.7) | copy-start | bytes 12582916
  106.2 1.0 copy-start.3
  106.2 1.1 copy-start.4
  106.2 1.3 copy-start.5
  107.5 10.3 %slice-start = ((s8[8388608]{0:T(1024)(128)(4,1)}), s8[4194304]{0:T(1024)(128)(4,1)S(1)}, s32[]{:S(2)}) async-start(s8[8388608]{0:T(1024)(128)(4,1)} %bitcast.60), calls=%async_computation.4 | async-start | bytes 8388608
  109.9 7.9 %copy-start.2 = (bf16[1,256,8192]{2,1,0:T(8,128)(2,1)S(1)}, bf16[1,256,8192]{2,1,0:T(8,128)(2,1)}, u32[]{:S(2)}) copy-start(bf16[1,256,8192]{2,1,0:T(8,128)(2,1)} %param.7) | copy-start | bytes 12582916
  109.9 7.9 %slice-start.1 = ((s8[8388608]{0:T(1024)(128)(4,1)}), s8[4194304]{0:T(1024)(128)(4,1)S(1)}, s32[]{:S(2)}) async-start(s8[8388608]{0:T(1024)(128)(4,1)} %bitcast.60), calls=%async_computation.5 | async-start | bytes 8388608
Sparse Core Ops, SparseCore 0:
  10.7 75.2 all-gather.1
  106.4 144.0 reduce-scatter.1
Sparse Core Ops, SparseCore 1:
  12.4 89.9 all-reduce.1
where the time goes:
time: 258 us
  waiting for transfers between devices  204 us (79%)
  matrix products  28.1 us (11%)
  between operations  15.5 us (6%)
  other arithmetic  8.93 us (3%)
    reduce_scatter x1, waiting for transfers between devices, body(): lax.psum_scatter(jnp.einsum('td,tk->dk', normed, cotangent, preferred_ele...  129 us
    all_gather x1, waiting for transfers between devices, body(): gathered = lax.all_gather(key_weight, 'fsdp', axis=1, tiled=True)[0]  74.3 us
    dot_general x1, matrix products, body(): jnp.einsum('tk,dk->td', cotangent, gathered, preferred_element_type=jnp.f...  11.9 us
    dot_general x1, matrix products, body(): jnp.einsum('td,tk->dk', normed, cotangent, preferred_element_type=jnp.flo...  8.27 us
    dot_general x1, matrix products, body(): key_sum = jnp.dot(normed, gathered, preferred_element_type=jnp.float32)  7.88 us
  transfers between devices with their start and end apart: 3, of which 2 were waited for; matrix products, arithmetic and copies ran while one was open for 14% of the time, Pallas kernels for 0%

commit v1 on v0

v1 whole, which is shorter than its diff:
```python
import jax
import jax.numpy as jnp
from jax import lax
from jax.experimental import pallas as pl
from jax.experimental.pallas import tpu as pltpu
from jax.sharding import PartitionSpec as P

epsilon = 1e-05
outer_rate = 0.7
outer_momentum = 0.9
mix_weight = 0.5

MESH = pl.DeviceIdType.MESH
F32 = jnp.float32
BF16 = jnp.bfloat16

D = 8192
KC = 512
TOK = 256
NZ = 8
ISLANDS = 8
NCHIP = 16
HALF = 128
SIGNS = (1, -1)


def norm_dz(dz):
    dz = dz % NZ
    return dz - NZ if dz > 4 else dz


def copy_names():
    names = []
    for d in (0, 1):
        for k in (1, 2, 3, 4):
            for dy in (0, 1):
                if k <= chain_len(d, dy):
                    names += [("gA", d, dy, k), ("rA", d, dy, k)]
            names += [("gB", d, k), ("rB", d, k)]
    names += [("gyA",), ("ryA",), ("own",), ("cot",), ("n", 0), ("n", 1)]
    for dz in range(-3, 5):
        names += [("gyB", dz), ("ryB", dz)]
        for dy in (0, 1):
            if (dy, dz) != (0, 0):
                names += [("sA", dy, dz), ("sB", dy, dz)]
    for j in (1, 2, 3):
        names += [("fx", j), ("ft", j)]
    names += [("fy",)]
    return {name: i for i, name in enumerate(names)}


def chain_len(d, dy):
    return 4 if d == dy else 3


NAMES = copy_names()


def kernel(
    hid_h, gain_h, w_h, cot_h, fg_h, fm_h, fl_h,
    keys_o, gi_o, gw_o, ng_o, nm_o, nl_o,
    w, hid, nrm, nsib, upper, part, gain, cot, cot_t, kacc, iacc, scl,
    fg, fm, fl, fx, fs, ftot,
    r_a, st_a, yb_s, yb_r, r_b, st_b, ya_s, ya_r,
    ssem, rsem, lsem,
):
    island = lax.axis_index("island")
    f = lax.axis_index("fsdp")
    c = lax.rem(f, 2)
    z = lax.rem(lax.div(f, 2), NZ)
    y = lax.div(f, 2 * NZ)
    x = lax.rem(island, 4)
    yh = lax.div(island, 4)

    def fsdp_of(yy, zz, cc):
        return (yy * NZ + zz) * 2 + cc

    def q_of(dy, dz):
        yy = y if dy == 0 else 1 - y
        return yy * NZ + lax.rem(z + (dz + NZ), NZ)

    zdev = [
        (island, fsdp_of(y, lax.rem(z + 1, NZ), c)),
        (island, fsdp_of(y, lax.rem(z + NZ - 1, NZ), c)),
    ]
    ydev = (island, fsdp_of(1 - y, z, c))
    sdev = (island, fsdp_of(y, z, 1 - c))
    xdev = {j: (yh * 4 + lax.rem(x + j, 4), f) for j in (1, 2, 3)}
    hdev = ((1 - yh) * 4 + x, f)
    peers = zdev + [ydev, sdev, hdev] + [xdev[j] for j in (1, 2, 3)]

    sent = []

    def send(name, src, dst, dev):
        i = NAMES[name]
        copy = pltpu.make_async_remote_copy(
            src_ref=src, dst_ref=dst, send_sem=ssem.at[i], recv_sem=rsem.at[i],
            device_id=dev, device_id_type=MESH,
        )
        copy.start()
        sent.append(copy)

    def arrive(name, dst, dev):
        i = NAMES[name]
        pltpu.make_async_remote_copy(
            src_ref=dst, dst_ref=dst, send_sem=ssem.at[i], recv_sem=rsem.at[i],
            device_id=dev, device_id_type=MESH,
        ).wait_recv()

    loads = [
        (w_h.at[0], w.at[pl.ds(pl.multiple_of((y * NZ + z) * 512 + c * 256, 256), 256)]),
        (cot_h.at[0], cot.at[0]),
        (fl_h.at[0], fl),
        (gain_h, gain),
        (hid_h.at[0, pl.ds(0, 128)], hid.at[pl.ds(0, 128)]),
        (hid_h.at[0, pl.ds(128, 128)], hid.at[pl.ds(128, 128)]),
        (fg_h, fg),
        (fm_h, fm),
    ]
    local = [pltpu.make_async_copy(s, t, lsem.at[i]) for i, (s, t) in enumerate(loads)]
    for copy in local:
        copy.start()

    barrier = pltpu.get_barrier_semaphore()
    for dev in peers:
        pl.semaphore_signal(barrier, inc=1, device_id=dev, device_id_type=MESH)
    pl.semaphore_wait(barrier, len(peers))

    def wrows(dy, dz, start, size, core=None):
        core = c if core is None else core
        row = q_of(dy, dz) * 512 + core * 256 + start
        return w.at[pl.ds(pl.multiple_of(row, 32), size)]

    def b_span(d, k):
        if k < 4:
            return HALF, 256 - HALF
        half = (256 - HALF) // 2
        return (HALF, half) if d == 0 else (HALF + half, half)

    def g_send_a(d, dy, k):
        part_ = wrows(dy, norm_dz(-SIGNS[d] * (k - 1)), 0, HALF)
        send(("gA", d, dy, k), part_, part_, zdev[d])

    def g_send_b(d, k):
        start, size = b_span(d, k)
        part_ = wrows(0, norm_dz(-SIGNS[d] * (k - 1)), start, size)
        send(("gB", d, k), part_, part_, zdev[d])

    def g_send_yb(dz):
        part_ = wrows(0, dz, HALF, 256 - HALF)
        send(("gyB", dz), part_, part_, ydev)

    def to_sibling(which, dy, dz):
        start, size = (0, HALF) if which == "sA" else (HALF, 256 - HALF)
        part_ = wrows(dy, dz, start, size)
        send((which, dy, dz), part_, part_, sdev)

    def from_sibling(dy, dz):
        if (dy, dz) == (0, 0):
            arrive(("own",), wrows(0, 0, 0, 256, 1 - c), sdev)
            return
        arrive(("sA", dy, dz), wrows(dy, dz, 0, HALF, 1 - c), sdev)
        arrive(("sB", dy, dz), wrows(dy, dz, HALF, 256 - HALF, 1 - c), sdev)

    def g_recv_a(dy, k):
        for d in (0, 1):
            if k <= chain_len(d, dy):
                dz = norm_dz(-SIGNS[d] * k)
                arrive(("gA", d, dy, k), wrows(dy, dz, 0, HALF), zdev[d])
                if k < chain_len(d, dy):
                    g_send_a(d, dy, k + 1)
                to_sibling("sA", dy, dz)

    def g_recv_b(k):
        for d in (0, 1):
            dz = norm_dz(-SIGNS[d] * k)
            start, size = b_span(d, k)
            arrive(("gB", d, k), wrows(0, dz, start, size), zdev[d])
            if k < 4:
                g_send_b(d, k + 1)
            if k < 4 or d == 1:
                g_send_yb(dz)
                to_sibling("sB", 0, dz)

    def g_recv_yb(dz):
        arrive(("gyB", dz), wrows(1, dz, HALF, 256 - HALF), ydev)
        to_sibling("sB", 1, dz)

    def norm_block(i, carry):
        rows = pl.ds(pl.multiple_of(i * 32, 32), 32)
        acc = jnp.zeros((32, 512), F32)
        for j in range(16):
            h = hid[rows, j * 512:(j + 1) * 512].astype(F32)
            acc = acc + h * h
        total = jnp.sum(acc, axis=-1, keepdims=True)
        s = lax.rsqrt(total / D + epsilon)
        scl[rows, :] = s
        for j in range(16):
            h = hid[rows, j * 512:(j + 1) * 512].astype(F32)
            g = gain[:, j * 512:(j + 1) * 512].astype(F32)
            n = (h * s * g).astype(BF16)
            nrm[0, rows, j * 256:(j + 1) * 256] = n[:, :256]
            nrm[1, rows, j * 256:(j + 1) * 256] = n[:, 256:]
        return carry

    def norm_half(i):
        lax.fori_loop(i * 4, i * 4 + 4, norm_block, 0)
        rows = pl.ds(i * 128, 128)
        send(("n", i), nrm.at[1 - c, rows], nsib.at[rows], sdev)

    def part_block(q, carry):
        cols = pl.ds(pl.multiple_of(q * 256, 256), 256)
        a = jnp.dot(cot_t[0], nrm[c, :, cols], preferred_element_type=F32)
        b = jnp.dot(cot_t[1], nsib[:, cols], preferred_element_type=F32)
        part[q] = a + b
        return carry

    def work_on(q):
        cols = pl.ds(pl.multiple_of(q * 512, 512), 512)
        half = pl.ds(pl.multiple_of(q * 256, 256), 256)
        rows = pl.multiple_of(q * 512, 512)
        w0 = w[pl.ds(rows, 256), :]
        w1 = w[pl.ds(rows + 256, 256), :]
        kacc[...] += jnp.dot(nrm[0, :, half], w0, preferred_element_type=F32) + jnp.dot(
            nrm[1, :, half], w1, preferred_element_type=F32
        )
        back = lax.dot_general(
            cot[0], w[pl.ds(rows, 512), :], (((1,), (1,)), ((), ())), preferred_element_type=F32
        )
        u = back * gain[:, cols].astype(F32)
        upper[:, cols] = u
        t = u * hid[:, cols].astype(F32)
        iacc[...] += (t[:, :128] + t[:, 128:256]) + (t[:, 256:384] + t[:, 384:])

    def work_round(d):
        if d == 0 or d == 4:
            for dy in (0, 1):
                from_sibling(dy, d)
            lax.fori_loop(0, 2, lambda i, carry: (work_on(lax.rem(y + i, 2) * NZ + lax.rem(z + d, NZ)), carry)[1], 0)
            return
        for dz in (d, -d):
            for dy in (0, 1):
                from_sibling(dy, dz)

        def one(i, carry):
            zz = lax.rem(z + NZ + d - 2 * d * lax.div(i, 2), NZ)
            work_on(lax.rem(y + lax.rem(i, 2), 2) * NZ + zz)
            return carry

        lax.fori_loop(0, 4, one, 0)

    def add_into(dst, terms, rows, step=64):
        def one(i, carry):
            r = pl.ds(pl.multiple_of(i * step, step), step)
            total = terms[0][r, :].astype(F32)
            for term in terms[1:]:
                total = total + term[r, :].astype(F32)
            dst[r, :] = total.astype(dst.dtype)
            return carry

        lax.fori_loop(0, rows // step, one, 0)

    def p_rows(dy, dz, start, size):
        return part.at[q_of(dy, dz), pl.ds(start, size)]

    def r_send_yb(dz):
        slot = dz + 3
        add_into(yb_s.at[slot], [p_rows(1, dz, 256, 256)], 256)
        send(("ryB", dz), yb_s.at[slot], yb_r.at[slot], ydev)

    def r_step_a(t, dy):
        for d in (0, 1):
            if t == 1 and chain_len(d, dy) == 3:
                continue
            dz = norm_dz(SIGNS[d] * (5 - t))
            mine = p_rows(dy, dz, 0, 256)
            if t == 1 or (t == 2 and chain_len(d, dy) == 3):
                buf = st_a.at[d, dy]
                add_into(buf, [mine], 256)
            else:
                buf = r_a.at[d, dy, t - 2]
                arrive(("rA", d, dy, r_index(d, dy, t - 1)), buf, zdev[d])
                add_into(buf, [buf, mine], 256)
            send(("rA", d, dy, r_index(d, dy, t)), buf, r_a.at[d, dy, t - 1], zdev[d])

    def r_index(d, dy, t):
        return t - (4 - chain_len(d, dy))

    def r_step_b(t):
        for d in (0, 1):
            dz = norm_dz(SIGNS[d] * (5 - t))
            slot = dz + 3
            if t == 1:
                if d == 0:
                    arrive(("ryB", dz), yb_r.at[slot], ydev)
                start = d * 128
                add_into(
                    st_b.at[d],
                    [p_rows(0, dz, 256 + start, 128), yb_r.at[slot, pl.ds(start, 128)]], 128,
                )
                send(("rB", d, 1), st_b.at[d], r_b.at[d, 0, pl.ds(start, 128)], zdev[d])
                continue
            arrive(("ryB", dz), yb_r.at[slot], ydev)
            buf = r_b.at[d, t - 2]
            if t == 2:
                start = d * 128
                other = 128 - start
                add_into(
                    buf.at[pl.ds(other, 128)],
                    [p_rows(0, dz, 256 + other, 128), yb_r.at[slot, pl.ds(other, 128)]], 128,
                )
                arrive(("rB", d, 1), buf.at[pl.ds(start, 128)], zdev[d])
                add_into(
                    buf.at[pl.ds(start, 128)],
                    [buf.at[pl.ds(start, 128)], p_rows(0, dz, 256 + start, 128), yb_r.at[slot, pl.ds(start, 128)]],
                    128,
                )
            else:
                arrive(("rB", d, t - 1), buf, zdev[d])
                add_into(buf, [buf, p_rows(0, dz, 256, 256), yb_r.at[slot]], 256)
            send(("rB", d, t), buf, r_b.at[d, t - 1], zdev[d])

    def r_last_a(dy):
        for d in (0, 1):
            arrive(("rA", d, dy, r_index(d, dy, 4)), r_a.at[d, dy, 3], zdev[d])
        return [p_rows(dy, 0, 0, 256), r_a.at[0, dy, 3], r_a.at[1, dy, 3]]

    def write_gw(start, terms):
        for i in range(2):
            r = slice(i * 128, (i + 1) * 128)
            total = terms[0][r, :].astype(F32)
            for term in terms[1:]:
                total = total + term[r, :].astype(F32)
            gw_o[0, :, start + i * 128:start + (i + 1) * 128] = total.T

    for i in range(3):
        local[i].wait()
    send(("gyA",), wrows(0, 0, 0, HALF), wrows(0, 0, 0, HALF), ydev)
    for d in (0, 1):
        g_send_a(d, 0, 1)
    for d in (0, 1):
        g_send_b(d, 1)
    g_send_yb(0)
    send(("own",), wrows(0, 0, 0, 256), wrows(0, 0, 0, 256), sdev)
    send(("cot",), cot.at[0], cot.at[1], sdev)
    for j in (1, 2, 3):
        quarter = pl.ds(pl.multiple_of(lax.rem(x + j, 4) * 64, 64), 64)
        send(("fx", j), fl.at[quarter], fx.at[j - 1], xdev[j])

    kacc[...] = jnp.zeros_like(kacc)
    iacc[...] = jnp.zeros_like(iacc)
    cot_t[0] = cot[0].T

    local[3].wait()
    local[4].wait()
    norm_half(0)
    arrive(("gyA",), wrows(1, 0, 0, HALF), ydev)
    for d in (0, 1):
        g_send_a(d, 1, 1)
    to_sibling("sA", 1, 0)
    local[5].wait()
    norm_half(1)
    g_recv_yb(0)
    g_recv_a(0, 1)
    g_recv_b(1)
    g_recv_a(1, 1)

    arrive(("cot",), cot.at[1], sdev)
    cot_t[1] = cot[1].T
    for i in (0, 1):
        arrive(("n", i), nsib.at[pl.ds(i * 128, 128)], sdev)
    lax.fori_loop(0, NCHIP, part_block, 0)
    for dz in (4, 3, -3):
        r_send_yb(dz)
    r_step_a(1, 1)
    r_step_a(1, 0)

    g_recv_a(0, 2)
    g_recv_b(2)
    g_recv_a(1, 2)
    for dz in (1, -1):
        g_recv_yb(dz)
    r_step_b(1)

    mine64 = pl.ds(pl.multiple_of(x * 64, 64), 64)
    total = fl[mine64, :].astype(F32)
    others = []
    for j in (1, 2, 3):
        arrive(("fx", j), fx.at[j - 1], xdev[j])
        others.append(fx[j - 1].astype(F32))
    fs[0] = (total + others[1]) + (others[0] + others[2])
    send(("fy",), fs.at[0], fs.at[1], hdev)

    work_round(0)

    g_recv_a(0, 3)
    g_recv_b(3)
    g_recv_a(1, 3)
    for dz in (2, -2):
        r_send_yb(dz)
        g_recv_yb(dz)
    r_step_a(2, 1)
    r_step_a(2, 0)
    r_step_b(2)

    work_round(1)

    arrive(("fy",), fs.at[1], hdev)
    ftot[mine64, :] = (fs[0] + fs[1]) / ISLANDS
    for j in (1, 2, 3):
        send(("ft", j), ftot.at[mine64], ftot.at[mine64], xdev[j])

    g_recv_a(0, 4)
    g_recv_b(4)
    g_recv_a(1, 4)
    for dz in (1, -1, 0):
        r_send_yb(dz)
    r_step_a(3, 1)
    r_step_a(3, 0)
    r_step_b(3)

    work_round(2)

    for j in (1, 2, 3):
        quarter = pl.ds(pl.multiple_of(lax.rem(x + 4 - j, 4) * 64, 64), 64)
        arrive(("ft", j), ftot.at[quarter], xdev[j])
    local[6].wait()
    local[7].wait()

    def outer(i, carry):
        r = pl.ds(pl.multiple_of(i * 32, 32), 32)
        g = fg[r, :]
        pseudo = g - ftot[r, :]
        moment = outer_momentum * fm[r, :] + pseudo
        new = g - outer_rate * (pseudo + outer_momentum * moment)
        nm_o[r, :] = moment
        ng_o[r, :] = new
        nl_o[0, r, :] = (mix_weight * fl[r, :].astype(F32) + (1.0 - mix_weight) * new).astype(BF16)
        return carry

    lax.fori_loop(0, 8, outer, 0)

    for dz in (3, -3, 4):
        g_recv_yb(dz)
    r_step_a(4, 1)
    r_step_a(4, 0)
    r_step_b(4)

    work_round(3)
    work_round(4)
    keys_o[0] = kacc[...].astype(BF16)

    def finish(i, carry):
        r = pl.ds(pl.multiple_of(i * 32, 32), 32)
        s = scl[r, :]
        inner = jnp.sum(iacc[r, :], axis=-1, keepdims=True) / D
        coef = s * s * s * inner
        for j in range(16):
            cols = slice(j * 512, (j + 1) * 512)
            gi_o[0, r, cols] = (s * upper[r, cols] - hid[r, cols].astype(F32) * coef).astype(BF16)
        return carry

    lax.fori_loop(0, 8, finish, 0)

    add_into(ya_s, r_last_a(1), 256)
    send(("ryA",), ya_s, ya_r, ydev)
    arrive(("ryB", 0), yb_r.at[3], ydev)
    for d in (0, 1):
        arrive(("rB", d, 4), r_b.at[d, 3], zdev[d])
    write_gw(256, [p_rows(0, 0, 256, 256), yb_r.at[3], r_b.at[0, 3], r_b.at[1, 3]])
    terms = r_last_a(0)
    arrive(("ryA",), ya_r, ydev)
    write_gw(0, terms + [ya_r])

    for copy in sent:
        copy.wait_send()


def store(*refs):
    n = (len(refs) - 1) // 2
    copies = [pltpu.make_async_copy(refs[i], refs[n + i], refs[-1].at[i]) for i in range(n)]
    for copy in copies:
        copy.start()
    for copy in copies:
        copy.wait()


def body(*args):
    outs = [
        ((1, TOK, KC), BF16),
        ((1, TOK, D), BF16),
        ((1, TOK, KC), F32),
        ((TOK, KC), F32),
        ((TOK, KC), F32),
        ((1, TOK, KC), BF16),
    ]
    vm = pltpu.VMEM
    results = pl.pallas_call(
        kernel,
        out_shape=[vm(*o) for o in outs],
        in_specs=[pl.BlockSpec(memory_space=pltpu.HBM)] * 7,
        out_specs=[pl.BlockSpec(memory_space=vm)] * 6,
        scratch_shapes=[
            vm((D, KC), BF16),
            vm((TOK, D), BF16),
            vm((2, TOK, D // 2), BF16),
            vm((TOK, D // 2), BF16),
            vm((TOK, D), F32),
            vm((NCHIP, KC, 256), F32),
            vm((1, D), BF16),
            vm((2, TOK, KC), BF16),
            vm((2, KC, TOK), BF16),
            vm((TOK, KC), F32),
            vm((TOK, 128), F32),
            vm((TOK, 1), F32),
            vm((TOK, KC), F32),
            vm((TOK, KC), F32),
            vm((TOK, KC), BF16),
            vm((3, 64, KC), BF16),
            vm((2, 64, KC), F32),
            vm((TOK, KC), F32),
            vm((2, 2, 4, 256, 256), BF16),
            vm((2, 2, 256, 256), BF16),
            vm((8, 256, 256), BF16),
            vm((8, 256, 256), BF16),
            vm((2, 4, 256, 256), BF16),
            vm((2, 128, 256), BF16),
            vm((256, 256), BF16),
            vm((256, 256), BF16),
            pltpu.SemaphoreType.DMA((len(NAMES),)),
            pltpu.SemaphoreType.DMA((len(NAMES),)),
            pltpu.SemaphoreType.DMA((8,)),
        ],
        compiler_params=pltpu.CompilerParams(
            collective_id=0, has_side_effects=True, vmem_limit_bytes=56 * 2**20
        ),
    )(*args)
    return tuple(
        pl.pallas_call(
            store,
            out_shape=[jax.ShapeDtypeStruct(*o) for o in outs],
            in_specs=[pl.BlockSpec(memory_space=vm)] * 6,
            out_specs=[pl.BlockSpec(memory_space=pl.ANY)] * 6,
            scratch_shapes=[pltpu.SemaphoreType.DMA((6,))],
        )(*results)
    )


def solution(mesh):
    rows = P("island", "fsdp", None)
    frag = P("fsdp", None)
    return jax.shard_map(
        body,
        mesh=mesh,
        in_specs=(rows, P("island", None), rows, rows, frag, frag, rows),
        out_specs=(rows, rows, rows, frag, frag, rows),
        check_vma=False,
    )
```

time: 258 us -> 85.3 us (0.33)
  waiting for transfers between devices: 204 us -> 0 us
  Pallas kernels: 0 us -> 78.9 us
  matrix products: 28.1 us -> 0 us
  between operations: 15.5 us -> 0.66 us
  other arithmetic: 8.93 us -> 0 us
  local copies, waits for them, and re-layouts: 1.24 us -> 5.73 us
    reduce_scatter x1 -> x0, waiting for transfers between devices: 129 us -> none  [body(): lax.psum_scatter(jnp.einsum('td,tk->dk', normed, cotangent, preferred_ele...]
    pallas_call x0 -> x2, Pallas kernels: none -> 78.9 us  [the longest x1 73.4 us: body(): pl.pallas_call(kernel, out_shape=[vm(*o) for o in outs], in_specs=[pl.Blo...]
    all_gather x1 -> x0, waiting for transfers between devices: 74.3 us -> none  [body(): gathered = lax.all_gather(key_weight, 'fsdp', axis=1, tiled=True)[0]]
    dot_general x3 -> x0, matrix products: 28.1 us -> none  [the longest x1 11.9 us: body(): jnp.einsum('tk,dk->td', cotangent, gathered, preferred_element_type=jnp.f...]
    broadcast_in_dim x2 -> x0, other arithmetic: 6.15 us -> none  [the longest x1 3.72 us: body(): grad_in[None]]
    unnamed x16 -> x12, local copies, waits for them, and re-layouts: 1.24 us -> 5.73 us
  transfers between devices with their start and end apart: 3 -> 0, of which waited for: 2 -> 0; matrix products, arithmetic and copies ran while one was open for 14% -> 0% of each run, Pallas kernels for 0% -> 0%
where the time goes in v1:
time: 85.3 us
  Pallas kernels  78.9 us (92%)
  local copies, waits for them, and re-layouts  5.73 us (7%)
    pallas_call x1, Pallas kernels, body(): pl.pallas_call(kernel, out_shape=[vm(*o) for o in outs], in_specs=[pl.Blo...  73.4 us
    unnamed x12, local copies, waits for them, and re-layouts  5.73 us
    pallas_call x1, Pallas kernels, body(): pl.pallas_call(store, out_shape=[jax.ShapeDtypeStruct(*o) for o in outs],...  5.45 us

profile of v1, /device:TPU:2, one launch (start us, length us, event | category | flops | bytes accessed | tf_op | source)
XLA Modules:
  0.0 85.3 jit_solution(16294392565632093667)
XLA Ops:
  0.6 73.4 %shard_map.118 = (bf16[1,256,512]{2,1,0:T(8,128)(2,1)S(1)}, bf16[1,256,8192]{2,1,0:T(8,128)(2,1)S(1)}, f32[1,256,512]{2,1,0:T(8,128)S(1)}, f32[256,512]{1,0:T(8,...) custom-call(bf16[1,256,8192]{2,1,0:T(8,128)(2,1)} %hid_h.1, bf16[1,8192]{1,0:T(2,128)(2,1)} %gain_h.1, ...), custom_call_target="tpu_custom_call" | custom-call | tf_op jit(solution)/shard_map/pallas_call | solution.py:498
  74.1 0.0 copy-start
  74.1 1.9 %copy-done = bf16[1,256,8192]{2,1,0:T(8,128)(2,1)} copy-done((bf16[1,256,8192]{2,1,0:T(8,128)(2,1)}, bf16[1,256,8192]{2,1,0:T(8,128)(2,1)S(1)}, u32[]{:S(2)}) %copy-start) | copy-done | bytes 4194328
  76.0 0.0 copy-start.1
  76.0 0.8 copy-done.1
  76.8 0.0 copy-start.2
  76.8 0.8 copy-done.2
  77.6 0.0 copy-start.3
  77.6 0.8 copy-done.3
  78.4 0.0 copy-start.4
  78.4 0.7 copy-done.4
  79.1 0.0 copy-start.5
  79.1 0.7 copy-done.5
  79.8 5.4 %shard_map.119 = (bf16[1,256,512]{2,1,0:T(8,128)(2,1)}, bf16[1,256,8192]{2,1,0:T(8,128)(2,1)}, f32[1,256,512]{2,1,0:T(8,128)}, f32[256,512]{1,0:T(8,128)}, f32[2...) custom-call(bf16[1,256,512]{2,1,0:T(8,128)(2,1)} %copy-done.4, bf16[1,256,8192]{2,1,0:T(8,128)(2,1)} %copy-done, ...), custom_call_target="tpu_custom_call" | custom-call | tf_op jit(solution)/shard_map/pallas_call | solution.py:539
Async XLA Ops:
  74.1 1.9 %copy-start = (bf16[1,256,8192]{2,1,0:T(8,128)(2,1)}, bf16[1,256,8192]{2,1,0:T(8,128)(2,1)S(1)}, u32[]{:S(2)}) copy-start(bf16[1,256,8192]{2,1,0:T(8,128)(2,1)S(1)} %get-tuple-element.13.refs_1_) | copy-start | bytes 12582916
  76.0 0.8 copy-start.1
  76.8 0.8 copy-start.2
  77.6 0.8 copy-start.3
  78.4 0.7 copy-start.4
  79.1 0.7 copy-start.5

commit v2 on v1

--- a/solution.py
+++ b/solution.py
@@ -539,9 +539,10 @@
         pl.pallas_call(
             store,
             out_shape=[jax.ShapeDtypeStruct(*o) for o in outs],
-            in_specs=[pl.BlockSpec(memory_space=vm)] * 6,
+            in_specs=[pl.BlockSpec(memory_space=pl.ANY)] * 6,
             out_specs=[pl.BlockSpec(memory_space=pl.ANY)] * 6,
             scratch_shapes=[pltpu.SemaphoreType.DMA((6,))],
+            compiler_params=pltpu.CompilerParams(vmem_limit_bytes=2**20),
         )(*results)
     )
 

time: 85.3 us -> 76.9 us (0.902)
  local copies, waits for them, and re-layouts: 5.73 us -> 0 us
  Pallas kernels: 78.9 us -> 76.1 us
    unnamed x12 -> x0, local copies, waits for them, and re-layouts: 5.73 us -> none
    pallas_call x1, Pallas kernels: 5.45 us -> 2.7 us  [body(): pl.pallas_call(store, out_shape=[jax.ShapeDtypeStruct(*o) for o in outs],...]
where the time goes in v2:
time: 76.9 us; the launch traced here: 76.8 us
  Pallas kernels  76.1 us (99%)
    pallas_call x1, Pallas kernels, body(): pl.pallas_call(kernel, out_shape=[vm(*o) for o in outs], in_specs=[pl.Blo...  73.4 us
    pallas_call x1, Pallas kernels, body(): pl.pallas_call(store, out_shape=[jax.ShapeDtypeStruct(*o) for o in outs],...  2.7 us

profile of v2, /device:TPU:2, one launch (start us, length us, event | category | flops | bytes accessed | tf_op | source)
XLA Modules:
  0.0 76.8 jit_solution(11443372567089341040)
XLA Ops:
  0.6 73.4 %shard_map.118 = (bf16[1,256,512]{2,1,0:T(8,128)(2,1)S(1)}, bf16[1,256,8192]{2,1,0:T(8,128)(2,1)S(1)}, f32[1,256,512]{2,1,0:T(8,128)S(1)}, f32[256,512]{1,0:T(8,...) custom-call(bf16[1,256,8192]{2,1,0:T(8,128)(2,1)} %hid_h.1, bf16[1,8192]{1,0:T(2,128)(2,1)} %gain_h.1, ...), custom_call_target="tpu_custom_call" | custom-call | tf_op jit(solution)/shard_map/pallas_call | solution.py:498
  74.1 2.7 %shard_map.119 = (bf16[1,256,512]{2,1,0:T(8,128)(2,1)}, bf16[1,256,8192]{2,1,0:T(8,128)(2,1)}, f32[1,256,512]{2,1,0:T(8,128)}, f32[256,512]{1,0:T(8,128)}, f32[2...) custom-call(bf16[1,256,512]{2,1,0:T(8,128)(2,1)S(1)} %get-tuple-element.12.refs_0_, ...), custom_call_target="tpu_custom_call" | custom-call | tf_op jit(solution)/shard_map/pallas_call | solution.py:539

commit v3 on v2

v3 whole, which is shorter than its diff:
```python
import math

import jax
import jax.numpy as jnp
from jax import lax
from jax.experimental import pallas as pl
from jax.experimental.pallas import tpu as pltpu
from jax.sharding import PartitionSpec as P

epsilon = 1e-05
outer_rate = 0.7
outer_momentum = 0.9
mix_weight = 0.5

MESH = pl.DeviceIdType.MESH
F32 = jnp.float32
BF16 = jnp.bfloat16

D = 8192
KC = 512
TOK = 256
NZ = 8
ISLANDS = 8
NCHIP = 16
HALF = 112
SIGNS = (1, -1)


def norm_dz(dz):
    dz = dz % NZ
    return dz - NZ if dz > 4 else dz


def chain_len(d, dy):
    return 4 if d == dy else 3


def arrival(name):
    kind = name[0]
    if kind in ("own", "sA", "sB"):
        return ("s", name[2] if len(name) > 1 else 0)
    if kind in ("cot", "n"):
        return ("n",)
    if kind in ("fx", "ft"):
        return (kind,)
    if kind in ("gB", "rB") and name[2] == 4:
        return (kind, 4)
    if kind == "rA" and name[3] == 4:
        return (kind, 4, name[2])
    return name


def arrivals():
    names = [("gyA",), ("ryA",), ("n",), ("fx",), ("fy",), ("fz",), ("ft",), ("gB", 4), ("rB", 4)]
    for dy in (0, 1):
        names += [("rA", 4, dy)]
        for d in (0, 1):
            names += [("gA", d, dy, k) for k in range(1, 1 + chain_len(d, dy))]
            names += [("rA", d, dy, t) for t in range(5 - chain_len(d, dy), 4)]
    for k in (1, 2, 3):
        names += [(kind, d, k) for kind in ("gB", "rB") for d in (0, 1)]
    for dz in range(-3, 5):
        names += [(kind, dz) for kind in ("gyB", "ryB", "s")]
    return {name: i for i, name in enumerate(names)}


ARRIVALS = arrivals()

ORDER = (
    ("start",), ("norm", 0), ("norm", 1), ("gB", 0, 1), ("gyA",), ("gB", 1, 1), ("gB", 0, 2), ("gA", 1, 1, 1),
    ("part", 0), ("ryB", 4), ("rA", 0, 1, 2), ("rA", 0, 0, 1), ("gB", 1, 2), ("rA", 1, 1, 1), ("gA", 1, 0, 1),
    ("gyB", -1), ("part", 1), ("rA", 0, 1, 3), ("gA", 0, 1, 1), ("rA", 1, 0, 2), ("rB", 1, 1), ("gA", 0, 0, 1),
    ("fx",), ("gB", 1, 3), ("part", 2), ("gyB", 2), ("rA", 1, 1, 2), ("ryB", -3), ("gA", 1, 0, 2), ("rA", 0, 0, 2),
    ("gyB", 1), ("ryB", 3), ("gA", 1, 1, 2), ("gB", 0, 3), ("part", 3), ("ryB", -2), ("gyB", -2), ("rA", 1, 0, 3),
    ("gA", 0, 1, 2), ("pair", -1), ("fy",), ("pair", 1), ("gB", 1, 4), ("rB", 0, 1), ("gA", 0, 0, 2), ("rA", 1, 1, 3),
    ("gyB", 0), ("fz",), ("gA", 1, 1, 3), ("gA", 1, 0, 3), ("rB", 0, 2), ("gA", 0, 0, 3), ("rB", 1, 2), ("ryB", 2),
    ("rA", 0, 0, 3), ("gA", 0, 1, 3), ("gyB", 3), ("gyB", -3), ("pair", 2), ("rA", 1, 1, 4), ("rA", 0, 1, 4),
    ("ryB", 1), ("ft",), ("gyB", 4), ("pair", 0), ("ryB", -1), ("pair", -2), ("rB", 1, 3), ("gA", 1, 1, 4),
    ("gA", 0, 0, 4), ("rB", 0, 3), ("pair", 3), ("rA", 1, 0, 4), ("rA", 0, 0, 4), ("ryB", 0), ("pair", -3),
    ("pair", 4), ("fin", 0), ("rB", 1, 4), ("ryA",), ("rB", 0, 4), ("fin", 1), ("fin", 2), ("fin", 3), ("endA",),
    ("endB",),
)

GROUPS = ((4, 3), (-3, 2), (-2, 1), (-1, 0))


def kernel(
    hid_h, gain_h, w_h, cot_h, fg_h, fm_h, fl_h,
    keys_o, gi_o, gw_o, ng_o, nm_o, nl_o,
    w, hid, nrm, nsib, upper, part, gain, cot, cot_t, kacc, iacc, scl,
    fg, fm, fl, fx, fs, ftot,
    r_a, st_a, yb_s, yb_r, r_b, st_b, ya_s, ya_r,
    ssem, rsem, lsem,
):
    island = lax.axis_index("island")
    f = lax.axis_index("fsdp")
    c = lax.rem(f, 2)
    z = lax.rem(lax.div(f, 2), NZ)
    y = lax.div(f, 2 * NZ)
    x = lax.rem(island, 4)
    yh = lax.div(island, 4)

    def fsdp_of(yy, zz, cc):
        return (yy * NZ + zz) * 2 + cc

    def q_of(dy, dz):
        yy = y if dy == 0 else 1 - y
        return yy * NZ + lax.rem(z + (dz + NZ), NZ)

    zdev = [
        (island, fsdp_of(y, lax.rem(z + 1, NZ), c)),
        (island, fsdp_of(y, lax.rem(z + NZ - 1, NZ), c)),
    ]
    ydev = (island, fsdp_of(1 - y, z, c))
    sdev = (island, fsdp_of(y, z, 1 - c))
    xdev = {j: (yh * 4 + lax.rem(x + j, 4), f) for j in (1, 2, 3)}
    hdev = ((1 - yh) * 4 + x, fsdp_of(1 - y, z, c))
    peers = zdev + [ydev, sdev, hdev] + [xdev[j] for j in (1, 2, 3)]

    sent = [0, 0]

    def send(name, src, dst, dev):
        group = 0 if name[0] in ("own", "gA", "gB", "gyA", "gyB", "sA", "sB") else 1
        pltpu.make_async_remote_copy(
            src_ref=src, dst_ref=dst, send_sem=ssem.at[group], recv_sem=rsem.at[ARRIVALS[arrival(name)]],
            device_id=dev, device_id_type=MESH,
        ).start()
        sent[group] += math.prod(src.shape) * src.dtype.itemsize

    def arrive(name, ref, dev):
        pltpu.make_async_remote_copy(
            src_ref=ref, dst_ref=ref, send_sem=ssem.at[0], recv_sem=rsem.at[ARRIVALS[name]],
            device_id=dev, device_id_type=MESH,
        ).wait_recv()

    loads = [
        (w_h.at[0], w.at[pl.ds(pl.multiple_of((y * NZ + z) * 512 + c * 256, 256), 256)]),
        (cot_h.at[0], cot.at[0]),
        (fl_h.at[0], fl),
        (gain_h, gain),
        (hid_h.at[0, pl.ds(0, 128)], hid.at[pl.ds(0, 128)]),
        (hid_h.at[0, pl.ds(128, 128)], hid.at[pl.ds(128, 128)]),
        (fg_h, fg),
        (fm_h, fm),
    ]
    local = [pltpu.make_async_copy(s, t, lsem.at[i]) for i, (s, t) in enumerate(loads)]
    for copy in local:
        copy.start()

    barrier = pltpu.get_barrier_semaphore()
    for dev in peers:
        pl.semaphore_signal(barrier, inc=1, device_id=dev, device_id_type=MESH)
    pl.semaphore_wait(barrier, len(peers))

    def wrows(dy, dz, start, size, core=None):
        core = c if core is None else core
        row = q_of(dy, dz) * 512 + core * 256 + start
        return w.at[pl.ds(pl.multiple_of(row, 16), size)]

    def b_span(d, k):
        if k < 4:
            return HALF, 256 - HALF
        half = (256 - HALF) // 32 * 16
        first = 256 - HALF - half
        return (HALF, first) if d == 0 else (HALF + first, half)

    def g_send_a(d, dy, k):
        part_ = wrows(dy, norm_dz(-SIGNS[d] * (k - 1)), 0, HALF)
        send(("gA", d, dy, k), part_, part_, zdev[d])

    def g_send_b(d, k):
        start, size = b_span(d, k)
        part_ = wrows(0, norm_dz(-SIGNS[d] * (k - 1)), start, size)
        send(("gB", d, k), part_, part_, zdev[d])

    def g_send_yb(dz):
        part_ = wrows(0, dz, HALF, 256 - HALF)
        send(("gyB", dz), part_, part_, ydev)

    def to_sibling(which, dy, dz):
        start, size = (0, HALF) if which == "sA" else (HALF, 256 - HALF)
        part_ = wrows(dy, dz, start, size)
        send((which, dy, dz), part_, part_, sdev)

    def step_start():
        for i in range(2):
            local[i].wait()
        send(("gyA",), wrows(0, 0, 0, HALF), wrows(0, 0, 0, HALF), ydev)
        for d in (0, 1):
            g_send_b(d, 1)
        g_send_yb(0)
        for d in (0, 1):
            g_send_a(d, 0, 1)
        send(("own",), wrows(0, 0, 0, 256), wrows(0, 0, 0, 256), sdev)
        send(("cot",), cot.at[0], cot.at[1], sdev)
        local[2].wait()
        for j in (1, 2, 3):
            quarter = pl.ds(pl.multiple_of(lax.rem(x + j, 4) * 64, 64), 64)
            send(("fx", j), fl.at[quarter], fx.at[j - 1], xdev[j])
        kacc[...] = jnp.zeros_like(kacc)
        iacc[...] = jnp.zeros_like(iacc)
        cot_t[0] = cot[0].T

    def step_gya():
        arrive(("gyA",), wrows(1, 0, 0, HALF), ydev)
        for d in (0, 1):
            g_send_a(d, 1, 1)
        to_sibling("sA", 1, 0)

    def step_ga(d, dy, k):
        dz = norm_dz(-SIGNS[d] * k)
        arrive(("gA", d, dy, k), wrows(dy, dz, 0, HALF), zdev[d])
        if k < chain_len(d, dy):
            g_send_a(d, dy, k + 1)
        to_sibling("sA", dy, dz)

    def step_gb(d, k):
        dz = norm_dz(-SIGNS[d] * k)
        if k == 4:
            arrive(("gB", 4), wrows(0, dz, HALF, 256 - HALF), zdev[d])
        else:
            arrive(("gB", d, k), wrows(0, dz, HALF, 256 - HALF), zdev[d])
            g_send_b(d, k + 1)
        g_send_yb(dz)
        to_sibling("sB", 0, dz)

    def step_gyb(dz):
        arrive(("gyB", dz), wrows(1, dz, HALF, 256 - HALF), ydev)
        to_sibling("sB", 1, dz)

    def norm_block(i, carry):
        rows = pl.ds(pl.multiple_of(i * 32, 32), 32)
        acc = jnp.zeros((32, 512), F32)
        for j in range(16):
            h = hid[rows, j * 512:(j + 1) * 512].astype(F32)
            acc = acc + h * h
        total = jnp.sum(acc, axis=-1, keepdims=True)
        s = lax.rsqrt(total / D + epsilon)
        scl[rows, :] = s
        for j in range(16):
            h = hid[rows, j * 512:(j + 1) * 512].astype(F32)
            g = gain[:, j * 512:(j + 1) * 512].astype(F32)
            n = (h * s * g).astype(BF16)
            nrm[0, rows, j * 256:(j + 1) * 256] = n[:, :256]
            nrm[1, rows, j * 256:(j + 1) * 256] = n[:, 256:]
        return carry

    def step_norm(i):
        if i == 0:
            local[3].wait()
        local[4 + i].wait()
        lax.fori_loop(i * 4, i * 4 + 4, norm_block, 0)
        rows = pl.ds(i * 128, 128)
        send(("n", i), nrm.at[1 - c, rows], nsib.at[rows], sdev)

    def step_part(p):
        if p == 0:
            arrive(("n",), w.at[pl.ds(0, 2304)], sdev)
            cot_t[1] = cot[1].T
        first, second = GROUPS[p]

        def one(i, carry):
            zz = lax.rem(z + NZ + first + (second - first) * lax.div(i, 2), NZ)
            q = lax.rem(y + lax.rem(i, 2), 2) * NZ + zz
            cols = pl.ds(pl.multiple_of(q * 256, 256), 256)
            a = jnp.dot(cot_t[0], nrm[c, :, cols], preferred_element_type=F32)
            b = jnp.dot(cot_t[1], nsib[:, cols], preferred_element_type=F32)
            part[q] = a + b
            return carry

        lax.fori_loop(0, 4, one, 0)

    def work_on(q):
        cols = pl.ds(pl.multiple_of(q * 512, 512), 512)
        half = pl.ds(pl.multiple_of(q * 256, 256), 256)
        rows = pl.multiple_of(q * 512, 512)
        w0 = w[pl.ds(rows, 256), :]
        w1 = w[pl.ds(rows + 256, 256), :]
        kacc[...] += jnp.dot(nrm[0, :, half], w0, preferred_element_type=F32) + jnp.dot(
            nrm[1, :, half], w1, preferred_element_type=F32
        )
        back = lax.dot_general(
            cot[0], w[pl.ds(rows, 512), :], (((1,), (1,)), ((), ())), preferred_element_type=F32
        )
        u = back * gain[:, cols].astype(F32)
        upper[:, cols] = u
        t = u * hid[:, cols].astype(F32)
        iacc[...] += (t[:, :128] + t[:, 128:256]) + (t[:, 256:384] + t[:, 384:])

    def step_pair(dz):
        arrive(("s", dz), w.at[pl.ds(pl.multiple_of(q_of(0, dz) * 512, 512), 512)], sdev)

        def one(i, carry):
            work_on(lax.rem(y + i, 2) * NZ + lax.rem(z + NZ + dz, NZ))
            return carry

        lax.fori_loop(0, 2, one, 0)

    def add_into(dst, terms, rows, step=64):
        def one(i, carry):
            r = pl.ds(pl.multiple_of(i * step, step), step)
            total = terms[0][r, :].astype(F32)
            for term in terms[1:]:
                total = total + term[r, :].astype(F32)
            dst[r, :] = total.astype(dst.dtype)
            return carry

        lax.fori_loop(0, rows // step, one, 0)

    def p_rows(dy, dz, start, size):
        return part.at[q_of(dy, dz), pl.ds(start, size)]

    def step_ryb(dz):
        slot = dz + 3
        add_into(yb_s.at[slot], [p_rows(1, dz, 256, 256)], 256)
        send(("ryB", dz), yb_s.at[slot], yb_r.at[slot], ydev)

    def step_ra(d, dy, t):
        dz = norm_dz(SIGNS[d] * (5 - t))
        mine = p_rows(dy, dz, 0, 256)
        if t == 5 - chain_len(d, dy):
            buf = st_a.at[d, dy]
            add_into(buf, [mine], 256)
        else:
            buf = r_a.at[d, dy, t - 2]
            arrive(("rA", d, dy, t - 1), buf, zdev[d])
            add_into(buf, [buf, mine], 256)
        send(("rA", d, dy, t), buf, r_a.at[d, dy, t - 1], zdev[d])

    def arrive_yb(dz):
        arrive(("ryB", dz), yb_r.at[dz + 3], ydev)

    def step_rb(d, t):
        dz = norm_dz(SIGNS[d] * (5 - t))
        slot = dz + 3
        start = d * 128
        other = 128 - start
        if t == 1:
            if not seen:
                arrive_yb(dz)
                seen.append(dz)
            add_into(
                st_b.at[d],
                [p_rows(0, dz, 256 + start, 128), yb_r.at[slot, pl.ds(start, 128)]], 128,
            )
            send(("rB", d, 1), st_b.at[d], r_b.at[d, 0, pl.ds(start, 128)], zdev[d])
            return
        arrive_yb(dz)
        buf = r_b.at[d, t - 2]
        if t == 2:
            arrive(("rB", d, 1), buf.at[pl.ds(start, 128)], zdev[d])
            add_into(
                buf.at[pl.ds(other, 128)],
                [p_rows(0, dz, 256 + other, 128), yb_r.at[slot, pl.ds(other, 128)]], 128,
            )
            add_into(
                buf.at[pl.ds(start, 128)],
                [buf.at[pl.ds(start, 128)], p_rows(0, dz, 256 + start, 128), yb_r.at[slot, pl.ds(start, 128)]],
                128,
            )
        else:
            arrive(("rB", d, t - 1), buf, zdev[d])
            add_into(buf, [buf, p_rows(0, dz, 256, 256), yb_r.at[slot]], 256)
        send(("rB", d, t), buf, r_b.at[d, t - 1], zdev[d])

    seen = []

    def last_a(dy):
        arrive(("rA", 4, dy), w.at[pl.ds(0, 256)], zdev[0])
        return [p_rows(dy, 0, 0, 256), r_a.at[0, dy, 3], r_a.at[1, dy, 3]]

    def write_gw(start, terms):
        for i in range(2):
            r = slice(i * 128, (i + 1) * 128)
            total = terms[0][r, :].astype(F32)
            for term in terms[1:]:
                total = total + term[r, :].astype(F32)
            gw_o[0, :, start + i * 128:start + (i + 1) * 128] = total.T

    def step_rya():
        add_into(ya_s, last_a(1), 256)
        send(("ryA",), ya_s, ya_r, ydev)

    def step_end_b():
        arrive_yb(0)
        arrive(("rB", 4), w.at[pl.ds(0, 256)], zdev[0])
        write_gw(256, [p_rows(0, 0, 256, 256), yb_r.at[3], r_b.at[0, 3], r_b.at[1, 3]])

    def step_end_a():
        terms = last_a(0)
        arrive(("ryA",), ya_r, ydev)
        write_gw(0, terms + [ya_r])

    mine64 = pl.ds(pl.multiple_of(x * 64, 64), 64)

    def step_fx():
        arrive(("fx",), w.at[pl.ds(0, 192)], xdev[1])
        others = [fx[j].astype(F32) for j in range(3)]
        fs[0] = (fl[mine64, :].astype(F32) + others[1]) + (others[0] + others[2])
        send(("fy",), fs.at[0], fs.at[1], ydev)

    def step_fy():
        arrive(("fy",), fs.at[1], ydev)
        send(("fz",), fs.at[1], fs.at[2], hdev)

    def step_fz():
        arrive(("fz",), fs.at[2], hdev)
        ftot[mine64, :] = (fs[0] + fs[2]) / ISLANDS
        for j in (1, 2, 3):
            send(("ft", j), ftot.at[mine64], ftot.at[mine64], xdev[j])

    def step_ft():
        arrive(("ft",), ftot.at[pl.ds(0, 192)], xdev[1])
        local[6].wait()
        local[7].wait()

        def outer(i, carry):
            r = pl.ds(pl.multiple_of(i * 32, 32), 32)
            g = fg[r, :]
            pseudo = g - ftot[r, :]
            moment = outer_momentum * fm[r, :] + pseudo
            new = g - outer_rate * (pseudo + outer_momentum * moment)
            nm_o[r, :] = moment
            ng_o[r, :] = new
            nl_o[0, r, :] = (mix_weight * fl[r, :].astype(F32) + (1.0 - mix_weight) * new).astype(BF16)
            return carry

        lax.fori_loop(0, 8, outer, 0)

    def step_fin(p):
        if p == 0:
            keys_o[0] = kacc[...].astype(BF16)

        def finish(i, carry):
            r = pl.ds(pl.multiple_of(i * 32, 32), 32)
            s = scl[r, :]
            inner = jnp.sum(iacc[r, :], axis=-1, keepdims=True) / D
            coef = s * s * s * inner
            for j in range(16):
                cols = slice(j * 512, (j + 1) * 512)
                gi_o[0, r, cols] = (s * upper[r, cols] - hid[r, cols].astype(F32) * coef).astype(BF16)
            return carry

        lax.fori_loop(2 * p, 2 * p + 2, finish, 0)

    steps = {
        "start": step_start, "gyA": step_gya, "gA": step_ga, "gB": step_gb, "gyB": step_gyb,
        "norm": step_norm, "part": step_part, "ryB": step_ryb, "rA": step_ra, "rB": step_rb,
        "fx": step_fx, "fy": step_fy, "fz": step_fz, "ft": step_ft, "pair": step_pair, "fin": step_fin,
        "ryA": step_rya, "endB": step_end_b, "endA": step_end_a,
    }
    for step in ORDER:
        steps[step[0]](*step[1:])

    for group in (0, 1):
        everything = w.at[pl.ds(0, sent[group] // (KC * 2))]
        pltpu.make_async_remote_copy(
            src_ref=everything, dst_ref=everything, send_sem=ssem.at[group], recv_sem=rsem.at[0],
            device_id=sdev, device_id_type=MESH,
        ).wait_send()


def store(*refs):
    n = (len(refs) - 1) // 2
    copies = [pltpu.make_async_copy(refs[i], refs[n + i], refs[-1].at[i]) for i in range(n)]
    for copy in copies:
        copy.start()
    for copy in copies:
        copy.wait()


def body(*args):
    outs = [
        ((1, TOK, KC), BF16),
        ((1, TOK, D), BF16),
        ((1, TOK, KC), F32),
        ((TOK, KC), F32),
        ((TOK, KC), F32),
        ((1, TOK, KC), BF16),
    ]
    vm = pltpu.VMEM
    results = pl.pallas_call(
        kernel,
        out_shape=[vm(*o) for o in outs],
        in_specs=[pl.BlockSpec(memory_space=pltpu.HBM)] * 7,
        out_specs=[pl.BlockSpec(memory_space=vm)] * 6,
        scratch_shapes=[
            vm((D, KC), BF16),
            vm((TOK, D), BF16),
            vm((2, TOK, D // 2), BF16),
            vm((TOK, D // 2), BF16),
            vm((TOK, D), F32),
            vm((NCHIP, KC, 256), F32),
            vm((1, D), BF16),
            vm((2, TOK, KC), BF16),
            vm((2, KC, TOK), BF16),
            vm((TOK, KC), F32),
            vm((TOK, 128), F32),
            vm((TOK, 1), F32),
            vm((TOK, KC), F32),
            vm((TOK, KC), F32),
            vm((TOK, KC), BF16),
            vm((3, 64, KC), BF16),
            vm((3, 64, KC), F32),
            vm((TOK, KC), F32),
            vm((2, 2, 4, 256, 256), BF16),
            vm((2, 2, 256, 256), BF16),
            vm((8, 256, 256), BF16),
            vm((8, 256, 256), BF16),
            vm((2, 4, 256, 256), BF16),
            vm((2, 128, 256), BF16),
            vm((256, 256), BF16),
            vm((256, 256), BF16),
            pltpu.SemaphoreType.DMA((2,)),
            pltpu.SemaphoreType.DMA((len(ARRIVALS),)),
            pltpu.SemaphoreType.DMA((8,)),
        ],
        compiler_params=pltpu.CompilerParams(
            collective_id=0, has_side_effects=True, vmem_limit_bytes=56 * 2**20
        ),
    )(*args)
    return tuple(
        pl.pallas_call(
            store,
            out_shape=[jax.ShapeDtypeStruct(*o) for o in outs],
            in_specs=[pl.BlockSpec(memory_space=pl.ANY)] * 6,
            out_specs=[pl.BlockSpec(memory_space=pl.ANY)] * 6,
            scratch_shapes=[pltpu.SemaphoreType.DMA((6,))],
            compiler_params=pltpu.CompilerParams(vmem_limit_bytes=2**20),
        )(*results)
    )


def solution(mesh):
    rows = P("island", "fsdp", None)
    frag = P("fsdp", None)
    return jax.shard_map(
        body,
        mesh=mesh,
        in_specs=(rows, P("island", None), rows, rows, frag, frag, rows),
        out_specs=(rows, rows, rows, frag, frag, rows),
        check_vma=False,
    )
```

time: 76.9 us -> 72.2 us (0.939)
  Pallas kernels: 76.1 us -> 71.5 us
    pallas_call x1, Pallas kernels: 73.4 us -> 68.8 us  [body(): pl.pallas_call(kernel, out_shape=[vm(*o) for o in outs], in_specs=[pl.Blo...]
where the time goes in v3:
time: 72.2 us; the launch traced here: 72.1 us
  Pallas kernels  71.5 us (99%)
    pallas_call x1, Pallas kernels, body(): pl.pallas_call(kernel, out_shape=[vm(*o) for o in outs], in_specs=[pl.Blo...  68.8 us
    pallas_call x1, Pallas kernels, body(): pl.pallas_call(store, out_shape=[jax.ShapeDtypeStruct(*o) for o in outs],...  2.7 us

profile of v3, /device:TPU:2, one launch (start us, length us, event | category | flops | bytes accessed | tf_op | source)
XLA Modules:
  0.0 72.1 jit_solution(1340122914479635308)
XLA Ops:
  0.6 68.8 %shard_map.118 = (bf16[1,256,512]{2,1,0:T(8,128)(2,1)S(1)}, bf16[1,256,8192]{2,1,0:T(8,128)(2,1)S(1)}, f32[1,256,512]{2,1,0:T(8,128)S(1)}, f32[256,512]{1,0:T(8,...) custom-call(bf16[1,256,8192]{2,1,0:T(8,128)(2,1)} %hid_h.1, bf16[1,8192]{1,0:T(2,128)(2,1)} %gain_h.1, ...), custom_call_target="tpu_custom_call" | custom-call | tf_op jit(solution)/shard_map/pallas_call | solution.py:482
  69.4 2.7 %shard_map.119 = (bf16[1,256,512]{2,1,0:T(8,128)(2,1)}, bf16[1,256,8192]{2,1,0:T(8,128)(2,1)}, f32[1,256,512]{2,1,0:T(8,128)}, f32[256,512]{1,0:T(8,128)}, f32[2...) custom-call(bf16[1,256,512]{2,1,0:T(8,128)(2,1)S(1)} %get-tuple-element.12.refs_0_, ...), custom_call_target="tpu_custom_call" | custom-call | tf_op jit(solution)/shard_map/pallas_call | solution.py:523

commit v4 on v3

--- a/solution.py
+++ b/solution.py
@@ -23,6 +23,9 @@
 ISLANDS = 8
 NCHIP = 16
 HALF = 112
+RA = 240
+RB = KC - RA
+RB0 = RB // 32 * 16 + RB % 32
 SIGNS = (1, -1)
 
 
@@ -67,18 +70,17 @@
 ARRIVALS = arrivals()
 
 ORDER = (
-    ("start",), ("norm", 0), ("norm", 1), ("gB", 0, 1), ("gyA",), ("gB", 1, 1), ("gB", 0, 2), ("gA", 1, 1, 1),
-    ("part", 0), ("ryB", 4), ("rA", 0, 1, 2), ("rA", 0, 0, 1), ("gB", 1, 2), ("rA", 1, 1, 1), ("gA", 1, 0, 1),
-    ("gyB", -1), ("part", 1), ("rA", 0, 1, 3), ("gA", 0, 1, 1), ("rA", 1, 0, 2), ("rB", 1, 1), ("gA", 0, 0, 1),
-    ("fx",), ("gB", 1, 3), ("part", 2), ("gyB", 2), ("rA", 1, 1, 2), ("ryB", -3), ("gA", 1, 0, 2), ("rA", 0, 0, 2),
-    ("gyB", 1), ("ryB", 3), ("gA", 1, 1, 2), ("gB", 0, 3), ("part", 3), ("ryB", -2), ("gyB", -2), ("rA", 1, 0, 3),
-    ("gA", 0, 1, 2), ("pair", -1), ("fy",), ("pair", 1), ("gB", 1, 4), ("rB", 0, 1), ("gA", 0, 0, 2), ("rA", 1, 1, 3),
-    ("gyB", 0), ("fz",), ("gA", 1, 1, 3), ("gA", 1, 0, 3), ("rB", 0, 2), ("gA", 0, 0, 3), ("rB", 1, 2), ("ryB", 2),
-    ("rA", 0, 0, 3), ("gA", 0, 1, 3), ("gyB", 3), ("gyB", -3), ("pair", 2), ("rA", 1, 1, 4), ("rA", 0, 1, 4),
-    ("ryB", 1), ("ft",), ("gyB", 4), ("pair", 0), ("ryB", -1), ("pair", -2), ("rB", 1, 3), ("gA", 1, 1, 4),
-    ("gA", 0, 0, 4), ("rB", 0, 3), ("pair", 3), ("rA", 1, 0, 4), ("rA", 0, 0, 4), ("ryB", 0), ("pair", -3),
-    ("pair", 4), ("fin", 0), ("rB", 1, 4), ("ryA",), ("rB", 0, 4), ("fin", 1), ("fin", 2), ("fin", 3), ("endA",),
-    ("endB",),
+    ("start",), ("norm", 0), ("norm", 1), ("gyA",), ("gB", 0, 1), ("gB", 1, 1), ("gA", 1, 0, 1), ("gA", 0, 1, 1),
+    ("fx",), ("part", 0), ("gA", 0, 0, 1), ("rA", 0, 0, 1), ("rA", 1, 1, 1), ("ryB", 4), ("gA", 1, 1, 1), ("part", 1),
+    ("gB", 1, 2), ("gyB", 0), ("gB", 0, 2), ("gA", 0, 1, 2), ("gyB", -1), ("gyB", 1), ("fy",), ("part", 2),
+    ("gA", 1, 0, 2), ("ryB", -3), ("rA", 0, 0, 2), ("gA", 0, 0, 2), ("pair", -1), ("rA", 0, 1, 2), ("gA", 1, 1, 2),
+    ("rA", 1, 0, 2), ("gB", 1, 3), ("fz",), ("pair", 0), ("gA", 0, 1, 3), ("ryB", 3), ("gyB", -2), ("gyB", 2),
+    ("rA", 1, 1, 2), ("rB", 0, 1), ("rB", 1, 1), ("gA", 1, 1, 3), ("gB", 0, 3), ("rA", 0, 1, 3), ("pair", 1),
+    ("rB", 0, 2), ("ryB", -2), ("gyB", 3), ("rA", 1, 1, 3), ("gB", 1, 4), ("gA", 0, 0, 3), ("rA", 1, 0, 3),
+    ("gyB", -3), ("ryB", 2), ("gA", 1, 0, 3), ("rB", 1, 2), ("rA", 0, 1, 4), ("gA", 1, 1, 4), ("part", 3), ("ft",),
+    ("ryB", -1), ("rA", 1, 1, 4), ("pair", 3), ("rA", 0, 0, 3), ("pair", -2), ("rB", 1, 3), ("ryB", 1), ("rB", 0, 3),
+    ("gA", 0, 0, 4), ("rA", 1, 0, 4), ("gyB", 4), ("ryA",), ("rA", 0, 0, 4), ("ryB", 0), ("pair", -3), ("pair", 4),
+    ("rB", 1, 4), ("rB", 0, 4), ("pair", 2), ("fin", 0), ("fin", 1), ("endA",), ("fin", 2), ("fin", 3), ("endB",),
 )
 
 GROUPS = ((4, 3), (-3, 2), (-2, 1), (-1, 0))
@@ -296,35 +298,39 @@
 
         lax.fori_loop(0, 2, one, 0)
 
-    def add_into(dst, terms, rows, step=64):
-        def one(i, carry):
-            r = pl.ds(pl.multiple_of(i * step, step), step)
+    def add_into(dst, terms, rows):
+        def some(r):
             total = terms[0][r, :].astype(F32)
             for term in terms[1:]:
                 total = total + term[r, :].astype(F32)
             dst[r, :] = total.astype(dst.dtype)
+
+        def one(i, carry):
+            some(pl.ds(pl.multiple_of(i * 64, 64), 64))
             return carry
 
-        lax.fori_loop(0, rows // step, one, 0)
+        lax.fori_loop(0, rows // 64, one, 0)
+        if rows % 64:
+            some(pl.ds(rows // 64 * 64, rows % 64))
 
     def p_rows(dy, dz, start, size):
         return part.at[q_of(dy, dz), pl.ds(start, size)]
 
     def step_ryb(dz):
         slot = dz + 3
-        add_into(yb_s.at[slot], [p_rows(1, dz, 256, 256)], 256)
+        add_into(yb_s.at[slot], [p_rows(1, dz, RA, RB)], RB)
         send(("ryB", dz), yb_s.at[slot], yb_r.at[slot], ydev)
 
     def step_ra(d, dy, t):
         dz = norm_dz(SIGNS[d] * (5 - t))
-        mine = p_rows(dy, dz, 0, 256)
+        mine = p_rows(dy, dz, 0, RA)
         if t == 5 - chain_len(d, dy):
             buf = st_a.at[d, dy]
-            add_into(buf, [mine], 256)
+            add_into(buf, [mine], RA)
         else:
             buf = r_a.at[d, dy, t - 2]
             arrive(("rA", d, dy, t - 1), buf, zdev[d])
-            add_into(buf, [buf, mine], 256)
+            add_into(buf, [buf, mine], RA)
         send(("rA", d, dy, t), buf, r_a.at[d, dy, t - 1], zdev[d])
 
     def arrive_yb(dz):
@@ -333,63 +339,59 @@
     def step_rb(d, t):
         dz = norm_dz(SIGNS[d] * (5 - t))
         slot = dz + 3
-        start = d * 128
-        other = 128 - start
+        spans = ((0, RB0), (RB0, RB - RB0))
+        start, size = spans[d]
+        span = pl.ds(start, size)
         if t == 1:
             if not seen:
                 arrive_yb(dz)
                 seen.append(dz)
-            add_into(
-                st_b.at[d],
-                [p_rows(0, dz, 256 + start, 128), yb_r.at[slot, pl.ds(start, 128)]], 128,
-            )
-            send(("rB", d, 1), st_b.at[d], r_b.at[d, 0, pl.ds(start, 128)], zdev[d])
+            buf = st_b.at[d, pl.ds(0, size)]
+            add_into(buf, [p_rows(0, dz, RA + start, size), yb_r.at[slot, span]], size)
+            send(("rB", d, 1), buf, r_b.at[d, 0, span], zdev[d])
             return
         arrive_yb(dz)
         buf = r_b.at[d, t - 2]
         if t == 2:
-            arrive(("rB", d, 1), buf.at[pl.ds(start, 128)], zdev[d])
-            add_into(
-                buf.at[pl.ds(other, 128)],
-                [p_rows(0, dz, 256 + other, 128), yb_r.at[slot, pl.ds(other, 128)]], 128,
-            )
-            add_into(
-                buf.at[pl.ds(start, 128)],
-                [buf.at[pl.ds(start, 128)], p_rows(0, dz, 256 + start, 128), yb_r.at[slot, pl.ds(start, 128)]],
-                128,
-            )
+            arrive(("rB", d, 1), buf.at[span], zdev[d])
+            add_into(buf.at[span], [buf.at[span], p_rows(0, dz, RA + start, size), yb_r.at[slot, span]], size)
+            start, size = spans[1 - d]
+            span = pl.ds(start, size)
+            add_into(buf.at[span], [p_rows(0, dz, RA + start, size), yb_r.at[slot, span]], size)
         else:
             arrive(("rB", d, t - 1), buf, zdev[d])
-            add_into(buf, [buf, p_rows(0, dz, 256, 256), yb_r.at[slot]], 256)
+            add_into(buf, [buf, p_rows(0, dz, RA, RB), yb_r.at[slot]], RB)
         send(("rB", d, t), buf, r_b.at[d, t - 1], zdev[d])
 
     seen = []
 
     def last_a(dy):
-        arrive(("rA", 4, dy), w.at[pl.ds(0, 256)], zdev[0])
-        return [p_rows(dy, 0, 0, 256), r_a.at[0, dy, 3], r_a.at[1, dy, 3]]
-
-    def write_gw(start, terms):
-        for i in range(2):
-            r = slice(i * 128, (i + 1) * 128)
-            total = terms[0][r, :].astype(F32)
-            for term in terms[1:]:
-                total = total + term[r, :].astype(F32)
-            gw_o[0, :, start + i * 128:start + (i + 1) * 128] = total.T
+        arrive(("rA", 4, dy), w.at[pl.ds(0, RA)], zdev[0])
+        return [p_rows(dy, 0, 0, RA), r_a.at[0, dy, 3], r_a.at[1, dy, 3]]
+
+    ended = []
+
+    def write_gw(block, terms, start, size):
+        mine = part.at[q_of(0, 0)]
+        add_into(mine.at[pl.ds(start, size)], terms, size)
+        blocks = (0,) if block == 0 else (2, 3)
+        for i in blocks + ((1,) if ended else ()):
+            gw_o[0, :, i * 128:(i + 1) * 128] = mine[pl.ds(i * 128, 128), :].T
+        ended.append(block)
 
     def step_rya():
-        add_into(ya_s, last_a(1), 256)
+        add_into(ya_s, last_a(1), RA)
         send(("ryA",), ya_s, ya_r, ydev)
 
     def step_end_b():
         arrive_yb(0)
-        arrive(("rB", 4), w.at[pl.ds(0, 256)], zdev[0])
-        write_gw(256, [p_rows(0, 0, 256, 256), yb_r.at[3], r_b.at[0, 3], r_b.at[1, 3]])
+        arrive(("rB", 4), w.at[pl.ds(0, RB)], zdev[0])
+        write_gw(2, [p_rows(0, 0, RA, RB), yb_r.at[3], r_b.at[0, 3], r_b.at[1, 3]], RA, RB)
 
     def step_end_a():
         terms = last_a(0)
         arrive(("ryA",), ya_r, ydev)
-        write_gw(0, terms + [ya_r])
+        write_gw(0, terms + [ya_r], 0, RA)
 
     mine64 = pl.ds(pl.multiple_of(x * 64, 64), 64)
 
@@ -503,14 +505,14 @@
             vm((3, 64, KC), BF16),
             vm((3, 64, KC), F32),
             vm((TOK, KC), F32),
-            vm((2, 2, 4, 256, 256), BF16),
-            vm((2, 2, 256, 256), BF16),
-            vm((8, 256, 256), BF16),
-            vm((8, 256, 256), BF16),
-            vm((2, 4, 256, 256), BF16),
-            vm((2, 128, 256), BF16),
-            vm((256, 256), BF16),
-            vm((256, 256), BF16),
+            vm((2, 2, 4, RA, 256), BF16),
+            vm((2, 2, RA, 256), BF16),
+            vm((8, RB, 256), BF16),
+            vm((8, RB, 256), BF16),
+            vm((2, 4, RB, 256), BF16),
+            vm((2, RB0, 256), BF16),
+            vm((RA, 256), BF16),
+            vm((RA, 256), BF16),
             pltpu.SemaphoreType.DMA((2,)),
             pltpu.SemaphoreType.DMA((len(ARRIVALS),)),
             pltpu.SemaphoreType.DMA((8,)),

time: 72.2 us -> 71.3 us (0.988)
  Pallas kernels: 71.5 us -> 70.6 us
    pallas_call x1, Pallas kernels: 68.8 us -> 67.9 us  [body(): pl.pallas_call(kernel, out_shape=[vm(*o) for o in outs], in_specs=[pl.Blo...]
where the time goes in v4:
time: 71.3 us; the launch traced here: 71.2 us
  Pallas kernels  70.6 us (99%)
    pallas_call x1, Pallas kernels, body(): pl.pallas_call(kernel, out_shape=[vm(*o) for o in outs], in_specs=[pl.Blo...  67.9 us
    pallas_call x1, Pallas kernels, body(): pl.pallas_call(store, out_shape=[jax.ShapeDtypeStruct(*o) for o in outs],...  2.7 us

profile of v4, /device:TPU:2, one launch (start us, length us, event | category | flops | bytes accessed | tf_op | source)
XLA Modules:
  0.0 71.2 jit_solution(10589690364164440498)
XLA Ops:
  0.6 67.9 %shard_map.118 = (bf16[1,256,512]{2,1,0:T(8,128)(2,1)S(1)}, bf16[1,256,8192]{2,1,0:T(8,128)(2,1)S(1)}, f32[1,256,512]{2,1,0:T(8,128)S(1)}, f32[256,512]{1,0:T(8,...) custom-call(bf16[1,256,8192]{2,1,0:T(8,128)(2,1)} %hid_h.1, bf16[1,8192]{1,0:T(2,128)(2,1)} %gain_h.1, ...), custom_call_target="tpu_custom_call" | custom-call | tf_op jit(solution)/shard_map/pallas_call | solution.py:484
  68.5 2.7 %shard_map.119 = (bf16[1,256,512]{2,1,0:T(8,128)(2,1)}, bf16[1,256,8192]{2,1,0:T(8,128)(2,1)}, f32[1,256,512]{2,1,0:T(8,128)}, f32[256,512]{1,0:T(8,128)}, f32[2...) custom-call(bf16[1,256,512]{2,1,0:T(8,128)(2,1)S(1)} %get-tuple-element.12.refs_0_, ...), custom_call_target="tpu_custom_call" | custom-call | tf_op jit(solution)/shard_map/pallas_call | solution.py:525

commit v5 on v4

--- a/solution.py
+++ b/solution.py
@@ -70,17 +70,19 @@
 ARRIVALS = arrivals()
 
 ORDER = (
-    ("start",), ("norm", 0), ("norm", 1), ("gyA",), ("gB", 0, 1), ("gB", 1, 1), ("gA", 1, 0, 1), ("gA", 0, 1, 1),
-    ("fx",), ("part", 0), ("gA", 0, 0, 1), ("rA", 0, 0, 1), ("rA", 1, 1, 1), ("ryB", 4), ("gA", 1, 1, 1), ("part", 1),
-    ("gB", 1, 2), ("gyB", 0), ("gB", 0, 2), ("gA", 0, 1, 2), ("gyB", -1), ("gyB", 1), ("fy",), ("part", 2),
-    ("gA", 1, 0, 2), ("ryB", -3), ("rA", 0, 0, 2), ("gA", 0, 0, 2), ("pair", -1), ("rA", 0, 1, 2), ("gA", 1, 1, 2),
-    ("rA", 1, 0, 2), ("gB", 1, 3), ("fz",), ("pair", 0), ("gA", 0, 1, 3), ("ryB", 3), ("gyB", -2), ("gyB", 2),
-    ("rA", 1, 1, 2), ("rB", 0, 1), ("rB", 1, 1), ("gA", 1, 1, 3), ("gB", 0, 3), ("rA", 0, 1, 3), ("pair", 1),
-    ("rB", 0, 2), ("ryB", -2), ("gyB", 3), ("rA", 1, 1, 3), ("gB", 1, 4), ("gA", 0, 0, 3), ("rA", 1, 0, 3),
-    ("gyB", -3), ("ryB", 2), ("gA", 1, 0, 3), ("rB", 1, 2), ("rA", 0, 1, 4), ("gA", 1, 1, 4), ("part", 3), ("ft",),
-    ("ryB", -1), ("rA", 1, 1, 4), ("pair", 3), ("rA", 0, 0, 3), ("pair", -2), ("rB", 1, 3), ("ryB", 1), ("rB", 0, 3),
-    ("gA", 0, 0, 4), ("rA", 1, 0, 4), ("gyB", 4), ("ryA",), ("rA", 0, 0, 4), ("ryB", 0), ("pair", -3), ("pair", 4),
-    ("rB", 1, 4), ("rB", 0, 4), ("pair", 2), ("fin", 0), ("fin", 1), ("endA",), ("fin", 2), ("fin", 3), ("endB",),
+    ("start",), ("norm", 0), ("tin", 0), ("norm", 1), ("tin", 1), ("gB", 0, 1), ("gB", 1, 1), ("tin", 2),
+    ("gA", 1, 0, 1), ("tin", 3), ("gyB", 0), ("gyA",), ("gA", 0, 0, 1), ("far",), ("gB", 0, 2), ("gB", 1, 2),
+    ("part", 0), ("tout", 0), ("part", 1), ("rA", 0, 0, 1), ("tout", 1), ("ryB", 4), ("rA", 1, 0, 2), ("gA", 1, 1, 1),
+    ("ryB", 3), ("tout", 2), ("gyB", -2), ("rA", 0, 1, 2), ("tout", 3), ("gB", 1, 3), ("tout", 4), ("gyB", 2),
+    ("gA", 0, 1, 1), ("gB", 0, 3), ("fl",), ("ryB", -3), ("rA", 1, 1, 1), ("rB", 0, 1), ("rA", 0, 0, 2), ("part", 2),
+    ("rB", 1, 1), ("part", 3), ("gA", 0, 1, 2), ("gA", 1, 1, 2), ("gyB", -1), ("rA", 1, 1, 2), ("gA", 1, 0, 2),
+    ("gA", 0, 0, 2), ("fx",), ("gyB", 3), ("pair", 2), ("rB", 0, 2), ("ryB", -2), ("ryB", 2), ("pair", 0),
+    ("gA", 1, 1, 3), ("rA", 1, 1, 3), ("gA", 1, 0, 3), ("rA", 0, 1, 3), ("fy",), ("gA", 0, 0, 3), ("gyB", 1),
+    ("gA", 0, 1, 3), ("gB", 1, 4), ("rB", 1, 2), ("rA", 0, 0, 3), ("pair", -1), ("rA", 1, 1, 4), ("pair", 3),
+    ("gA", 1, 1, 4), ("rA", 0, 1, 4), ("ryB", 1), ("ryB", -1), ("fz",), ("rA", 1, 0, 3), ("gyB", -3), ("pair", 1),
+    ("pair", -2), ("gA", 0, 0, 4), ("rB", 1, 3), ("rB", 0, 3), ("gyB", 4), ("rA", 0, 0, 4), ("rA", 1, 0, 4), ("ryA",),
+    ("ryB", 0), ("pair", -3), ("rB", 1, 4), ("rB", 0, 4), ("pair", 4), ("fin", 0), ("fin", 1), ("ft",), ("fin", 2),
+    ("endA",), ("fin", 3), ("endB",),
 )
 
 GROUPS = ((4, 3), (-3, 2), (-2, 1), (-1, 0))
@@ -92,7 +94,7 @@
     w, hid, nrm, nsib, upper, part, gain, cot, cot_t, kacc, iacc, scl,
     fg, fm, fl, fx, fs, ftot,
     r_a, st_a, yb_s, yb_r, r_b, st_b, ya_s, ya_r,
-    ssem, rsem, lsem,
+    ssem, rsem, lsem, in_sem, out_sem, far_sem,
 ):
     island = lax.axis_index("island")
     f = lax.axis_index("fsdp")
@@ -117,7 +119,25 @@
     sdev = (island, fsdp_of(y, z, 1 - c))
     xdev = {j: (yh * 4 + lax.rem(x + j, 4), f) for j in (1, 2, 3)}
     hdev = ((1 - yh) * 4 + x, fsdp_of(1 - y, z, c))
-    peers = zdev + [ydev, sdev, hdev] + [xdev[j] for j in (1, 2, 3)]
+    near = zdev + [ydev, sdev]
+    far = [hdev] + [xdev[j] for j in (1, 2, 3)]
+    dist = jnp.where(z > 4, NZ - z, z)
+    inner = (island, fsdp_of(y, jnp.where(z > 4, lax.rem(z + 1, NZ), lax.rem(z + NZ - 1, NZ)), c))
+    outer_z = jnp.where(z > 4, z - 1, lax.rem(z + 1, NZ))
+    outermost = (z == 4) | (z == 5)
+    outer = (island, fsdp_of(y, outer_z, c))
+
+    def signal(sem, dev):
+        pl.semaphore_signal(sem, inc=1, device_id=dev, device_id_type=MESH)
+
+    barrier = pltpu.get_barrier_semaphore()
+    for dev in near:
+        signal(barrier, dev)
+
+    @pl.when(z == 0)
+    def _():
+        for dev in far:
+            signal(barrier, dev)
 
     sent = [0, 0]
 
@@ -149,10 +169,13 @@
     for copy in local:
         copy.start()
 
-    barrier = pltpu.get_barrier_semaphore()
-    for dev in peers:
-        pl.semaphore_signal(barrier, inc=1, device_id=dev, device_id_type=MESH)
-    pl.semaphore_wait(barrier, len(peers))
+    @pl.when(z == 0)
+    def _():
+        pl.semaphore_wait(barrier, len(near) + len(far))
+
+    @pl.when(z != 0)
+    def _():
+        pl.semaphore_wait(barrier, len(near))
 
     def wrows(dy, dz, start, size, core=None):
         core = c if core is None else core
@@ -196,9 +219,6 @@
         send(("own",), wrows(0, 0, 0, 256), wrows(0, 0, 0, 256), sdev)
         send(("cot",), cot.at[0], cot.at[1], sdev)
         local[2].wait()
-        for j in (1, 2, 3):
-            quarter = pl.ds(pl.multiple_of(lax.rem(x + j, 4) * 64, 64), 64)
-            send(("fx", j), fl.at[quarter], fx.at[j - 1], xdev[j])
         kacc[...] = jnp.zeros_like(kacc)
         iacc[...] = jnp.zeros_like(iacc)
         cot_t[0] = cot[0].T
@@ -395,6 +415,35 @@
 
     mine64 = pl.ds(pl.multiple_of(x * 64, 64), 64)
 
+    def step_tin(i):
+        @pl.when(dist == 4 - i)
+        def _():
+            pl.when(jnp.logical_not(outermost))(lambda: pl.semaphore_wait(in_sem, 1))
+            signal(in_sem, inner)
+
+    def step_far():
+        @pl.when(z == 0)
+        def _():
+            pl.semaphore_wait(in_sem, 2)
+            for dev in far:
+                signal(far_sem, dev)
+
+    def step_tout(i):
+        @pl.when(dist == i)
+        def _():
+            if i == 0:
+                pl.semaphore_wait(far_sem, len(far))
+                for dev in zdev:
+                    signal(out_sem, dev)
+            else:
+                pl.semaphore_wait(out_sem, 1)
+                pl.when(jnp.logical_not(outermost))(lambda: signal(out_sem, outer))
+
+    def step_fl():
+        for j in (1, 2, 3):
+            quarter = pl.ds(pl.multiple_of(lax.rem(x + j, 4) * 64, 64), 64)
+            send(("fx", j), fl.at[quarter], fx.at[j - 1], xdev[j])
+
     def step_fx():
         arrive(("fx",), w.at[pl.ds(0, 192)], xdev[1])
         others = [fx[j].astype(F32) for j in range(3)]
@@ -416,7 +465,7 @@
         local[6].wait()
         local[7].wait()
 
-        def outer(i, carry):
+        def outer_step(i, carry):
             r = pl.ds(pl.multiple_of(i * 32, 32), 32)
             g = fg[r, :]
             pseudo = g - ftot[r, :]
@@ -427,7 +476,7 @@
             nl_o[0, r, :] = (mix_weight * fl[r, :].astype(F32) + (1.0 - mix_weight) * new).astype(BF16)
             return carry
 
-        lax.fori_loop(0, 8, outer, 0)
+        lax.fori_loop(0, 8, outer_step, 0)
 
     def step_fin(p):
         if p == 0:
@@ -448,7 +497,7 @@
     steps = {
         "start": step_start, "gyA": step_gya, "gA": step_ga, "gB": step_gb, "gyB": step_gyb,
         "norm": step_norm, "part": step_part, "ryB": step_ryb, "rA": step_ra, "rB": step_rb,
-        "fx": step_fx, "fy": step_fy, "fz": step_fz, "ft": step_ft, "pair": step_pair, "fin": step_fin,
+        "tin": step_tin, "far": step_far, "tout": step_tout, "fl": step_fl, "fx": step_fx, "fy": step_fy, "fz": step_fz, "ft": step_ft, "pair": step_pair, "fin": step_fin,
         "ryA": step_rya, "endB": step_end_b, "endA": step_end_a,
     }
     for step in ORDER:
@@ -516,6 +565,9 @@
             pltpu.SemaphoreType.DMA((2,)),
             pltpu.SemaphoreType.DMA((len(ARRIVALS),)),
             pltpu.SemaphoreType.DMA((8,)),
+            pltpu.SemaphoreType.REGULAR,
+            pltpu.SemaphoreType.REGULAR,
+            pltpu.SemaphoreType.REGULAR,
         ],
         compiler_params=pltpu.CompilerParams(
             collective_id=0, has_side_effects=True, vmem_limit_bytes=56 * 2**20

time: 71.3 us -> 69.9 us (0.980)
  Pallas kernels: 70.6 us -> 69.1 us
    pallas_call x1, Pallas kernels: 67.9 us -> 66.4 us  [body(): pl.pallas_call(kernel, out_shape=[vm(*o) for o in outs], in_specs=[pl.Blo...]
where the time goes in v5:
time: 69.9 us; the launch traced here: 69.8 us
  Pallas kernels  69.1 us (99%)
    pallas_call x1, Pallas kernels, body(): pl.pallas_call(kernel, out_shape=[vm(*o) for o in outs], in_specs=[pl.Blo...  66.4 us
    pallas_call x1, Pallas kernels, body(): pl.pallas_call(store, out_shape=[jax.ShapeDtypeStruct(*o) for o in outs],...  2.7 us

profile of v5, /device:TPU:2, one launch (start us, length us, event | category | flops | bytes accessed | tf_op | source)
XLA Modules:
  0.0 69.8 jit_solution(8900213931566972396)
XLA Ops:
  0.6 66.4 %shard_map.118 = (bf16[1,256,512]{2,1,0:T(8,128)(2,1)S(1)}, bf16[1,256,8192]{2,1,0:T(8,128)(2,1)S(1)}, f32[1,256,512]{2,1,0:T(8,128)S(1)}, f32[256,512]{1,0:T(8,...) custom-call(bf16[1,256,8192]{2,1,0:T(8,128)(2,1)} %hid_h.1, bf16[1,8192]{1,0:T(2,128)(2,1)} %gain_h.1, ...), custom_call_target="tpu_custom_call" | custom-call | tf_op jit(solution)/shard_map/pallas_call | solution.py:533
  67.1 2.7 %shard_map.119 = (bf16[1,256,512]{2,1,0:T(8,128)(2,1)}, bf16[1,256,8192]{2,1,0:T(8,128)(2,1)}, f32[1,256,512]{2,1,0:T(8,128)}, f32[256,512]{1,0:T(8,128)}, f32[2...) custom-call(bf16[1,256,512]{2,1,0:T(8,128)(2,1)S(1)} %get-tuple-element.12.refs_0_, ...), custom_call_target="tpu_custom_call" | custom-call | tf_op jit(solution)/shard_map/pallas_call | solution.py:577

commit v6 on v5

--- a/solution.py
+++ b/solution.py
@@ -208,17 +208,19 @@
         send((which, dy, dz), part_, part_, sdev)
 
     def step_start():
-        for i in range(2):
+        def own(name, start, size, dev):
+            send(name, w_h.at[0, pl.ds(start, size)], wrows(0, 0, start, size), dev)
+
+        for d in (0, 1):
+            own(("gB", d, 1), HALF, 256 - HALF, zdev[d])
+        own(("gyA",), 0, HALF, ydev)
+        own(("gyB", 0), HALF, 256 - HALF, ydev)
+        for d in (0, 1):
+            own(("gA", d, 0, 1), 0, HALF, zdev[d])
+        own(("own",), 0, 256, sdev)
+        send(("cot",), cot_h.at[0], cot.at[1], sdev)
+        for i in range(3):
             local[i].wait()
-        send(("gyA",), wrows(0, 0, 0, HALF), wrows(0, 0, 0, HALF), ydev)
-        for d in (0, 1):
-            g_send_b(d, 1)
-        g_send_yb(0)
-        for d in (0, 1):
-            g_send_a(d, 0, 1)
-        send(("own",), wrows(0, 0, 0, 256), wrows(0, 0, 0, 256), sdev)
-        send(("cot",), cot.at[0], cot.at[1], sdev)
-        local[2].wait()
         kacc[...] = jnp.zeros_like(kacc)
         iacc[...] = jnp.zeros_like(iacc)
         cot_t[0] = cot[0].T

time: 69.9 us -> 70.4 us (level)
  no operation moved by 1% of the time
where the time goes in v6:
time: 70.4 us; the launch traced here: 70 us
  Pallas kernels  69.3 us (98%)
    pallas_call x1, Pallas kernels, body(): pl.pallas_call(kernel, out_shape=[vm(*o) for o in outs], in_specs=[pl.Blo...  66.6 us
    pallas_call x1, Pallas kernels, body(): pl.pallas_call(store, out_shape=[jax.ShapeDtypeStruct(*o) for o in outs],...  2.7 us

profile of v6, /device:TPU:2, one launch (start us, length us, event | category | flops | bytes accessed | tf_op | source)
XLA Modules:
  0.0 70.0 jit_solution(4176495638144828756)
XLA Ops:
  0.6 66.6 %shard_map.118 = (bf16[1,256,512]{2,1,0:T(8,128)(2,1)S(1)}, bf16[1,256,8192]{2,1,0:T(8,128)(2,1)S(1)}, f32[1,256,512]{2,1,0:T(8,128)S(1)}, f32[256,512]{1,0:T(8,...) custom-call(bf16[1,256,8192]{2,1,0:T(8,128)(2,1)} %hid_h.1, bf16[1,8192]{1,0:T(2,128)(2,1)} %gain_h.1, ...), custom_call_target="tpu_custom_call" | custom-call | tf_op jit(solution)/shard_map/pallas_call | solution.py:535
  67.3 2.7 %shard_map.119 = (bf16[1,256,512]{2,1,0:T(8,128)(2,1)}, bf16[1,256,8192]{2,1,0:T(8,128)(2,1)}, f32[1,256,512]{2,1,0:T(8,128)}, f32[256,512]{1,0:T(8,128)}, f32[2...) custom-call(bf16[1,256,512]{2,1,0:T(8,128)(2,1)S(1)} %get-tuple-element.12.refs_0_, ...), custom_call_target="tpu_custom_call" | custom-call | tf_op jit(solution)/shard_map/pallas_call | solution.py:579
